TPU v7x, 32 devices: a whole 2x2x4 slice. The times are simulated.
32 devices in a mesh: frame: 8 (over z, x), head: 4 (over y, core).
Axes of the slice: x: 2, y: 2, z: 4, core: 2. Of those that a mesh axis runs over, the one named last changes fastest.
Arguments:
- query_proj: bfloat16 [16, 12288, 128], P('head', 'frame'), may hold values from -6 to 6
- key_proj: bfloat16 [16, 12288, 128], P('head', 'frame'), may hold values from -6 to 6
- value_proj: bfloat16 [16, 12288, 128], P('head', 'frame'), may hold values from -6 to 6
- lengths: int32 [16], replicated, may hold values from 384 to 1536, as said below
- out_weight: bfloat16 [1024, 1024], P('head'), may hold values from -0.1875 to 0.1875
Outputs:
- projected: bfloat16 [24576, 1024], P(('frame', 'head'))
Inputs may be any that keep to these rules, and one draw needn't show every extreme that they name: `lengths`: some frame has all 1536 tokens valid.
All inputs are finite; a program needn't handle non-finite values.
Results may differ from a plain program's by a relative error of at most 0.0057.
Values may be sent and summed in bfloat16 or wider, within the bound.
No kernel may reach another device: no remote copies, remote signals or barrier semaphores. Data moves between devices by JAX's collectives and lax.ppermute only.
A program may use at most 192 MiB of HBM per device.

v0:
```python
import math

import jax
import jax.numpy as jnp
from jax import lax
from jax.sharding import PartitionSpec as P

HS = 64
FT = 1536


def shifted(x, axis, by):
    length = lax.axis_size(axis)
    pairs = [(i, i + by) for i in range(length) if 0 <= i + by < length]
    return lax.ppermute(x, axis, pairs)


def frame_count(lengths, frame_id):
    table = jnp.arange(lengths.shape[0], dtype=jnp.int32)
    return jnp.sum(jnp.where(table == frame_id, lengths, 0))


def attend(queries, key_block, value_block, key_valid, local_heads):
    score_scale = 1.0 / math.sqrt(HS)
    block_rows = min(512, FT)
    block_count = FT // block_rows
    query_blocks = jnp.transpose(
        queries.reshape(local_heads, block_count, block_rows, HS), (1, 0, 2, 3)
    )

    def one_block(query_part):
        scores = (
            jnp.einsum("hqd,hkd->hqk", query_part, key_block, preferred_element_type=jnp.float32)
            * score_scale
        )
        scores = jnp.where(key_valid[None, None, :], scores, -jnp.inf)
        top_score = jnp.max(scores, axis=2, keepdims=True)
        expon = jnp.where(key_valid[None, None, :], jnp.exp(scores - top_score), 0.0)
        weights = (expon / jnp.sum(expon, axis=2, keepdims=True)).astype(jnp.bfloat16)
        result = jnp.einsum(
            "hqk,hkd->qhd", weights, value_block, preferred_element_type=jnp.float32
        )
        return result.astype(jnp.bfloat16).reshape(block_rows, local_heads * HS)

    return lax.map(one_block, query_blocks).reshape(FT, local_heads * HS)


def shards(query_proj, key_proj, value_proj, lengths, out_weight):
    local_heads = query_proj.shape[0]
    half_frame = FT // 2
    device_index = lax.axis_index("frame")
    stacked = jnp.stack((key_proj, value_proj))
    prev_frame_kv = shifted(stacked[:, :, half_frame:], "frame", 1)
    near_frames = shifted(stacked, "frame", 2)
    if lax.axis_size("frame") > 8:
        far_frames = shifted(stacked, "frame", 8)
    else:
        far_frames = jnp.zeros_like(stacked)
    positions = jnp.arange(FT, dtype=jnp.int32)
    outputs = []
    for within in range(2):
        frame_id = 2 * device_index + within
        lower = within * half_frame
        upper = (within + 1) * half_frame
        own_kv = stacked[:, :, lower:upper]
        before_kv = prev_frame_kv if within == 0 else stacked[:, :, :half_frame]
        gathered_kv = jnp.concatenate(
            (own_kv, before_kv, near_frames[:, :, lower:upper], far_frames[:, :, lower:upper]), 2
        )
        gathered_kv = gathered_kv.reshape(2, local_heads, 4 * FT, HS)
        sources = (frame_id, frame_id - 1, frame_id - 4, frame_id - 16)
        key_valid = jnp.concatenate(
            [positions < frame_count(lengths, source) for source in sources], 0
        )
        frame_queries = query_proj[:, lower:upper].reshape(local_heads, FT, HS)
        outputs.append(
            attend(frame_queries, gathered_kv[0], gathered_kv[1], key_valid, local_heads)
        )
    attended = jnp.concatenate(outputs, 0)
    token_rows = lax.all_to_all(attended, "head", split_axis=0, concat_axis=1, tiled=True)
    summed = jnp.dot(
        token_rows,
        lax.all_gather(out_weight, "head", axis=0, tiled=True),
        preferred_element_type=jnp.float32,
    )
    return summed.astype(jnp.bfloat16)


def solution(mesh):
    return jax.shard_map(
        shards,
        mesh=mesh,
        in_specs=(
            P("head", "frame", None),
            P("head", "frame", None),
            P("head", "frame", None),
            P(),
            P("head", None),
        ),
        out_specs=P(("frame", "head"), None),
        check_vma=False,
    )
```

profile of v0, /device:TPU:16, one launch (start us, length us, event | category | flops | bytes accessed | tf_op | source)
XLA Modules:
  0.0 797.8 jit_solution(7505711357775432578)
XLA Ops:
  37.7 44.8 %collective-permute-done.1 = bf16[2,4,1536,128]{3,2,1,0:T(8,128)(2,1)} collective-permute-done((bf16[2,4,1536,128]{3,2,1,0:T(8,128)(2,1)}, bf16[2,4,1536,128]{3,2,1,0:T(8,128)(2,1)}, u32[]{:S(2)}, u32[]{:S(2)}) %collective-permute-start.1) | collective-permute-done | bytes 3145760 | tf_op jit(solution)/shard_map/ppermute | solution.py:15
  84.7 32.5 %collective-permute-done = bf16[2,4,768,128]{3,2,1,0:T(8,128)(2,1)} collective-permute-done((bf16[2,4,768,128]{3,2,1,0:T(8,128)(2,1)S(1)}, bf16[2,4,768,128]{3,2,1,0:T(8,128)(2,1)}, u32[]{:S(2)}, u32[]{:S(2)}) %collective-permute-start) | collective-permute-done | bytes 1572896 | tf_op jit(solution)/shard_map/ppermute | solution.py:15
  117.2 10.1 %maximum_maximum_fusion = (bf16[2,4,3072,128]{3,2,1,0:T(8,128)(2,1)S(1)}, bf16[2,4,3072,128]{3,2,1,0:T(8,128)(2,1)S(1)}) fusion(bf16[2,4,768,128]{3,2,1,0:T(8,128)(2,1)S(1)} %get-tuple-element.122, bf16[2,4,768,128]{3,2,1,0:T(8,128)(2,1)} %collective-permute-done, bf16[2,4,768,128]{3,2,1,0:T(8,128)(2,1)S(1)} %get-tuple-element.125, ...), kind=kLoop, calls=%fused_computation.34 | loop fusion | flops 47185920 | bytes 20453376 | tf_op jit(solution)/shard_map/concatenate | solution.py:67
  131.1 5.4 squeeze.19
  136.5 5.2 copy.7
  141.7 8.8 %squeeze.20 = bf16[4,6144,64]{2,1,0:T(8,128)(2,1)} reshape(bf16[1,4,3072,128]{3,2,1,0:T(8,128)(2,1)} %get-tuple-element.118) | data formatting | bytes 6291456 | tf_op jit(solution)/shard_map/squeeze | solution.py:77
  150.5 6.7 copy.8
  158.2 285.3 %while.20 = (s32[]{:T(128)}, bf16[3,512,256]{2,1,0:T(8,128)(2,1)}, pred[6144]{0:T(1024)(128)(4,1)S(1)}, bf16[3,4,512,64]{2,3,1,0:T(8,128)(2,1)}, bf16[4,6144,64]...) while((s32[]{:T(128)}, bf16[3,512,256]{2,1,0:T(8,128)(2,1)}, ...), condition=%wide.region_7.8_spmd, body=%wide.region_4.7_spmd.sunk | while | flops 3334608896 | bytes 209214544 | solution.py:45
  158.2 20.3 %fusion.62 = f32[4,512,6144]{2,1,0:T(8,128)} fusion(bf16[4,6144,64]{1,2,0:T(8,128)(2,1)S(1)} %get-tuple-element.261, bf16[3,4,512,64]{2,3,1,0:T(8,128)(2,1)} %get-tuple-element.260, s32[]{:T(128)} %get-tuple-element.250), kind=kOutput, calls=%fused_computation.10.clone.1 | convolution fusion | flops 1610612736 | bytes 53740032 | tf_op jit(solution)/shard_map/while/body/eval_jaxpr/hqd,hkd->hqk/dot_general | solution.py:33
  178.4 53.2 %fusion.63 = (f32[4,512]{1,0:T(4,128)S(1)}, f32[4,512,6144]{2,1,0:T(8,128)}) fusion(f32[4,512,6144]{2,1,0:T(8,128)} %fusion.62, pred[6144]{0:T(1024)(128)(4,1)S(1)} %get-tuple-element.259), kind=kOutput, calls=%fused_computation.68.clone.1 | output fusion | flops 88086528 | bytes 100677632 | tf_op jit(solution)/shard_map/while/body/eval_jaxpr/sub | solution.py:38
  231.6 19.8 %fusion.64 = bf16[4,512,64]{1,2,0:T(8,128)(2,1)} fusion(bf16[4,6144,64]{1,2,0:T(8,128)(2,1)} %get-tuple-element.262, f32[4,512,6144]{2,1,0:T(8,128)} %get-tuple-element.212, f32[4,512]{1,0:T(4,128)S(1)} %get-tuple-element.213), kind=kOutput, calls=%fused_computation.9.clone.1 | convolution fusion | flops 1635909632 | bytes 53747712 | tf_op jit(solution)/shard_map/while/body/eval_jaxpr/hqk,hkd->qhd/dot_general | solution.py:40
  253.3 20.3 %fusion.62 = f32[4,512,6144]{2,1,0:T(8,128)} fusion(bf16[4,6144,64]{1,2,0:T(8,128)(2,1)S(1)} %get-tuple-element.261, bf16[3,4,512,64]{2,3,1,0:T(8,128)(2,1)} %get-tuple-element.260, s32[]{:T(128)} %get-tuple-element.250), kind=kOutput, calls=%fused_computation.10.clone.1 | convolution fusion | flops 1610612736 | bytes 53740032 | tf_op jit(solution)/shard_map/while/body/eval_jaxpr/hqd,hkd->hqk/dot_general | solution.py:33
  273.6 53.2 %fusion.63 = (f32[4,512]{1,0:T(4,128)S(1)}, f32[4,512,6144]{2,1,0:T(8,128)}) fusion(f32[4,512,6144]{2,1,0:T(8,128)} %fusion.62, pred[6144]{0:T(1024)(128)(4,1)S(1)} %get-tuple-element.259), kind=kOutput, calls=%fused_computation.68.clone.1 | output fusion | flops 88086528 | bytes 100677632 | tf_op jit(solution)/shard_map/while/body/eval_jaxpr/sub | solution.py:38
  326.8 19.8 %fusion.64 = bf16[4,512,64]{1,2,0:T(8,128)(2,1)} fusion(bf16[4,6144,64]{1,2,0:T(8,128)(2,1)} %get-tuple-element.262, f32[4,512,6144]{2,1,0:T(8,128)} %get-tuple-element.212, f32[4,512]{1,0:T(4,128)S(1)} %get-tuple-element.213), kind=kOutput, calls=%fused_computation.9.clone.1 | convolution fusion | flops 1635909632 | bytes 53747712 | tf_op jit(solution)/shard_map/while/body/eval_jaxpr/hqk,hkd->qhd/dot_general | solution.py:40
  348.4 20.3 %fusion.62 = f32[4,512,6144]{2,1,0:T(8,128)} fusion(bf16[4,6144,64]{1,2,0:T(8,128)(2,1)S(1)} %get-tuple-element.261, bf16[3,4,512,64]{2,3,1,0:T(8,128)(2,1)} %get-tuple-element.260, s32[]{:T(128)} %get-tuple-element.250), kind=kOutput, calls=%fused_computation.10.clone.1 | convolution fusion | flops 1610612736 | bytes 53740032 | tf_op jit(solution)/shard_map/while/body/eval_jaxpr/hqd,hkd->hqk/dot_general | solution.py:33
  368.7 53.2 %fusion.63 = (f32[4,512]{1,0:T(4,128)S(1)}, f32[4,512,6144]{2,1,0:T(8,128)}) fusion(f32[4,512,6144]{2,1,0:T(8,128)} %fusion.62, pred[6144]{0:T(1024)(128)(4,1)S(1)} %get-tuple-element.259), kind=kOutput, calls=%fused_computation.68.clone.1 | output fusion | flops 88086528 | bytes 100677632 | tf_op jit(solution)/shard_map/while/body/eval_jaxpr/sub | solution.py:38
  421.9 19.8 %fusion.64 = bf16[4,512,64]{1,2,0:T(8,128)(2,1)} fusion(bf16[4,6144,64]{1,2,0:T(8,128)(2,1)} %get-tuple-element.262, f32[4,512,6144]{2,1,0:T(8,128)} %get-tuple-element.212, f32[4,512]{1,0:T(4,128)S(1)} %get-tuple-element.213), kind=kOutput, calls=%fused_computation.9.clone.1 | convolution fusion | flops 1635909632 | bytes 53747712 | tf_op jit(solution)/shard_map/while/body/eval_jaxpr/hqk,hkd->qhd/dot_general | solution.py:40
  443.5 8.8 %squeeze.21 = bf16[4,6144,64]{2,1,0:T(8,128)(2,1)} reshape(bf16[1,4,3072,128]{3,2,1,0:T(8,128)(2,1)} %get-tuple-element.132) | data formatting | bytes 6291456 | tf_op jit(solution)/shard_map/squeeze | solution.py:77
  452.3 5.2 copy.11
  457.5 8.8 %squeeze.22 = bf16[4,6144,64]{2,1,0:T(8,128)(2,1)} reshape(bf16[1,4,3072,128]{3,2,1,0:T(8,128)(2,1)} %get-tuple-element.133) | data formatting | bytes 6291456 | tf_op jit(solution)/shard_map/squeeze | solution.py:77
  466.3 6.7 copy.12
  474.0 285.7 %while.21 = (s32[]{:T(128)}, bf16[3,512,256]{2,1,0:T(8,128)(2,1)}, pred[6144]{0:T(1024)(128)(4,1)S(1)}, bf16[3,4,512,64]{2,3,1,0:T(8,128)(2,1)}, bf16[4,6144,64]...) while((s32[]{:T(128)}, bf16[3,512,256]{2,1,0:T(8,128)(2,1)}, ...), condition=%wide.region_14.15_spmd, body=%wide.region_11.14_spmd.sunk | while | flops 3334608896 | bytes 209214544 | solution.py:45
  474.0 20.3 %fusion.68 = f32[4,512,6144]{2,1,0:T(8,128)} fusion(bf16[4,6144,64]{1,2,0:T(8,128)(2,1)S(1)} %get-tuple-element.240, bf16[3,4,512,64]{2,3,1,0:T(8,128)(2,1)} %get-tuple-element.239, s32[]{:T(128)} %get-tuple-element.229), kind=kOutput, calls=%fused_computation.27.clone.1 | convolution fusion | flops 1610612736 | bytes 53740032 | tf_op jit(solution)/shard_map/while/body/eval_jaxpr/hqd,hkd->hqk/dot_general | solution.py:33
  494.3 53.2 %fusion.69 = (f32[4,512]{1,0:T(4,128)S(1)}, f32[4,512,6144]{2,1,0:T(8,128)}) fusion(f32[4,512,6144]{2,1,0:T(8,128)} %fusion.68, pred[6144]{0:T(1024)(128)(4,1)S(1)} %get-tuple-element.238), kind=kOutput, calls=%fused_computation.69.clone.1 | output fusion | flops 88086528 | bytes 100677632 | tf_op jit(solution)/shard_map/while/body/eval_jaxpr/sub | solution.py:38
  547.6 19.8 %fusion.70 = bf16[4,512,64]{1,2,0:T(8,128)(2,1)} fusion(bf16[4,6144,64]{1,2,0:T(8,128)(2,1)} %get-tuple-element.241, f32[4,512,6144]{2,1,0:T(8,128)} %get-tuple-element.220, f32[4,512]{1,0:T(4,128)S(1)} %get-tuple-element.221), kind=kOutput, calls=%fused_computation.26.clone.1 | convolution fusion | flops 1635909632 | bytes 53747712 | tf_op jit(solution)/shard_map/while/body/eval_jaxpr/hqk,hkd->qhd/dot_general | solution.py:40
  569.2 20.3 %fusion.68 = f32[4,512,6144]{2,1,0:T(8,128)} fusion(bf16[4,6144,64]{1,2,0:T(8,128)(2,1)S(1)} %get-tuple-element.240, bf16[3,4,512,64]{2,3,1,0:T(8,128)(2,1)} %get-tuple-element.239, s32[]{:T(128)} %get-tuple-element.229), kind=kOutput, calls=%fused_computation.27.clone.1 | convolution fusion | flops 1610612736 | bytes 53740032 | tf_op jit(solution)/shard_map/while/body/eval_jaxpr/hqd,hkd->hqk/dot_general | solution.py:33
  589.6 53.2 %fusion.69 = (f32[4,512]{1,0:T(4,128)S(1)}, f32[4,512,6144]{2,1,0:T(8,128)}) fusion(f32[4,512,6144]{2,1,0:T(8,128)} %fusion.68, pred[6144]{0:T(1024)(128)(4,1)S(1)} %get-tuple-element.238), kind=kOutput, calls=%fused_computation.69.clone.1 | output fusion | flops 88086528 | bytes 100677632 | tf_op jit(solution)/shard_map/while/body/eval_jaxpr/sub | solution.py:38
  642.8 19.8 %fusion.70 = bf16[4,512,64]{1,2,0:T(8,128)(2,1)} fusion(bf16[4,6144,64]{1,2,0:T(8,128)(2,1)} %get-tuple-element.241, f32[4,512,6144]{2,1,0:T(8,128)} %get-tuple-element.220, f32[4,512]{1,0:T(4,128)S(1)} %get-tuple-element.221), kind=kOutput, calls=%fused_computation.26.clone.1 | convolution fusion | flops 1635909632 | bytes 53747712 | tf_op jit(solution)/shard_map/while/body/eval_jaxpr/hqk,hkd->qhd/dot_general | solution.py:40
  664.5 20.3 %fusion.68 = f32[4,512,6144]{2,1,0:T(8,128)} fusion(bf16[4,6144,64]{1,2,0:T(8,128)(2,1)S(1)} %get-tuple-element.240, bf16[3,4,512,64]{2,3,1,0:T(8,128)(2,1)} %get-tuple-element.239, s32[]{:T(128)} %get-tuple-element.229), kind=kOutput, calls=%fused_computation.27.clone.1 | convolution fusion | flops 1610612736 | bytes 53740032 | tf_op jit(solution)/shard_map/while/body/eval_jaxpr/hqd,hkd->hqk/dot_general | solution.py:33
  684.8 53.2 %fusion.69 = (f32[4,512]{1,0:T(4,128)S(1)}, f32[4,512,6144]{2,1,0:T(8,128)}) fusion(f32[4,512,6144]{2,1,0:T(8,128)} %fusion.68, pred[6144]{0:T(1024)(128)(4,1)S(1)} %get-tuple-element.238), kind=kOutput, calls=%fused_computation.69.clone.1 | output fusion | flops 88086528 | bytes 100677632 | tf_op jit(solution)/shard_map/while/body/eval_jaxpr/sub | solution.py:38
  738.0 19.8 %fusion.70 = bf16[4,512,64]{1,2,0:T(8,128)(2,1)} fusion(bf16[4,6144,64]{1,2,0:T(8,128)(2,1)} %get-tuple-element.241, f32[4,512,6144]{2,1,0:T(8,128)} %get-tuple-element.220, f32[4,512]{1,0:T(4,128)S(1)} %get-tuple-element.221), kind=kOutput, calls=%fused_computation.26.clone.1 | convolution fusion | flops 1635909632 | bytes 53747712 | tf_op jit(solution)/shard_map/while/body/eval_jaxpr/hqk,hkd->qhd/dot_general | solution.py:40
  766.4 20.0 %all-to-all-done = bf16[4,768,256]{1,2,0:T(8,128)(2,1)S(1)} async-done(((bf16[4,768,256]{1,2,0:T(8,128)(2,1)}), bf16[4,768,256]{1,2,0:T(8,128)(2,1)S(1)}, u32[]{:S(2)}, u32[]{:S(2)}) %all-to-all-start) | async-done | bytes 1572896 | tf_op jit(solution)/shard_map/all_to_all | solution.py:80
  (48 shorter events, 60.9 us)
Async XLA Ops:
  6.5 759.8 %all-gather.2.cloned.1.call-start = ((), (), s32[]{:S(2)}) async-start(), calls=%async_computation.1 | async-start | bytes 2621440 | tf_op jit(solution)/shard_map/all_gather | solution.py:83
  6.5 7.5 copy-start
  6.5 7.5 copy-start.1
  10.5 72.0 %collective-permute-start.1 = (bf16[2,4,1536,128]{3,2,1,0:T(8,128)(2,1)}, bf16[2,4,1536,128]{3,2,1,0:T(8,128)(2,1)}, u32[]{:S(2)}, u32[]{:S(2)}) collective-permute-start(bf16[2,4,1536,128]{3,2,1,0:T(8,128)(2,1)} %pad_maximum_fusion), channel_id=1, source_target_pairs={{0,8},{4,12},{8,16},{12,20},{16,24},{20,28},{1,9},{5,13},{9,17},{1... | collective-permute-start | bytes 9437192 | tf_op jit(solution)/shard_map/ppermute | solution.py:15
  14.4 102.8 %collective-permute-start = (bf16[2,4,768,128]{3,2,1,0:T(8,128)(2,1)S(1)}, bf16[2,4,768,128]{3,2,1,0:T(8,128)(2,1)}, u32[]{:S(2)}, u32[]{:S(2)}) collective-permute-start(bf16[2,4,768,128]{3,2,1,0:T(8,128)(2,1)S(1)} %get-tuple-element.124), channel_id=1, source_target_pairs={{0,4},{4,8},{8,12},{12,16},{16,20},{20,24},{24,28},{1,5},{5,9},{9,... | collective-permute-start | bytes 4718600 | tf_op jit(solution)/shard_map/ppermute | solution.py:15
  17.8 14.0 %copy-start.3 = (s32[16]{0:T(128)S(1)}, s32[16]{0:T(128)}, u32[]{:S(2)}) copy-start(s32[16]{0:T(128)} %param.12) | copy-start | bytes 196
  466.3 7.7 copy-start.2
  762.8 23.6 %all-to-all-start = ((bf16[4,768,256]{1,2,0:T(8,128)(2,1)}), bf16[4,768,256]{1,2,0:T(8,128)(2,1)S(1)}, u32[]{:S(2)}, u32[]{:S(2)}) async-start(bf16[4,768,256]{1,2,0:T(8,128)(2,1)} %copy.14), calls=%async_computation | async-start | bytes 3145728 | tf_op jit(solution)/shard_map/all_to_all | solution.py:80
Sparse Core Ops, SparseCore 0:
  17.9 22.4 all-gather.1
where the time goes:
time: 800 us; the launch traced here: 798 us
  other arithmetic  341 us (43%)
  matrix products  245 us (31%)
  waiting for transfers between devices  97.4 us (12%)
  local copies, waits for them, and re-layouts  89.8 us (11%)
  between operations  13.5 us (2%)
  starting transfers between devices  10.4 us (1%)
    sub x6, other arithmetic, one_block(): scores - top_score  319 us
    dot_general x6, matrix products, one_block(): jnp.einsum('hqd,hkd->hqk', query_part, key_block, preferred_element_type=...  122 us
    dot_general x6, matrix products, one_block(): jnp.einsum('hqk,hkd->qhd', weights, value_block, preferred_element_type=j...  119 us
    ppermute x2, waiting for transfers between devices, shifted(): return lax.ppermute(x, axis, pairs)  77.3 us
    while x6, local copies, waits for them, and re-layouts, attend(): return lax.map(one_block, query_blocks).reshape(FT, local_heads * HS)  28.7 us
    all_to_all x1, waiting for transfers between devices, shards(): lax.all_to_all(attended, 'head', split_axis=0, concat_axis=1, tiled=True)  20 us
    squeeze x2, local copies, waits for them, and re-layouts, shards(): gathered_kv[1]  17.6 us
  transfers between devices with their start and end apart: 4, of which 3 were waited for; matrix products, arithmetic and copies ran while one was open for 84% of the time, Pallas kernels for 0%

commit v1 on v0

v1 whole, which is shorter than its diff:
```python
import functools
import math

import jax
import jax.numpy as jnp
from jax import lax
from jax.experimental import pallas as pl
from jax.experimental.pallas import tpu as pltpu
from jax.sharding import PartitionSpec as P

LANES = 128
STRIDES = (0, 1, 4, 16)
VMEM = 48 * 1024 * 1024
LOW = -1e30


def swapped(x):
    return pltpu.roll(x, LANES // 2, 1)


def left_half(rows):
    return lax.broadcasted_iota(jnp.int32, (rows, LANES), 1) < LANES // 2


def split_queries(q_ref, q2_ref, scale):
    pairs = q_ref.shape[0]
    scaled = q_ref[...].astype(jnp.float32) * scale
    high = scaled.astype(jnp.bfloat16).astype(jnp.float32)
    low = scaled - high
    left = left_half(pairs)
    q2_ref[:pairs] = jnp.where(left, high, swapped(low)).astype(jnp.bfloat16)
    q2_ref[pairs:] = jnp.where(left, swapped(high), low).astype(jnp.bfloat16)


def key_rows(k_ref, start, pairs):
    block = k_ref[pl.ds(start, pairs), :].astype(jnp.float32)
    turned = swapped(block)
    left = left_half(pairs)
    even = jnp.where(left, block, turned)
    odd = jnp.where(left, turned, block)
    return jnp.concatenate([even, odd], axis=0).astype(jnp.bfloat16)


def value_rows(v_ref, start, pairs, count):
    block = v_ref[pl.ds(start, pairs), :].astype(jnp.float32)
    turned = swapped(block)
    lane = lax.broadcasted_iota(jnp.int32, (pairs, LANES), 1)
    token = 2 * (start + lax.broadcasted_iota(jnp.int32, (pairs, LANES), 0))
    left = lane < LANES // 2
    ones = (lane < 3 * LANES // 4).astype(jnp.float32)
    even = jnp.where(token < count, jnp.where(left, block, ones), 0.0)
    odd = jnp.where(token + 1 < count, jnp.where(left, turned, ones), 0.0)
    return jnp.concatenate([even, odd], axis=0).astype(jnp.bfloat16)


def over_tiles(count, pairs, step, body):
    half = step // 2
    halves = (count + 2 * half - 1) // (2 * half)
    whole = halves // 2

    def one(i, carry):
        body(pl.multiple_of(i * step, step), step)
        return carry

    lax.fori_loop(0, whole, one, 0)

    @pl.when(halves % 2 == 1)
    def _():
        body(pl.multiple_of(whole * step, step), half)


def scores_of(q2_ref, keys, at, rows):
    return lax.dot_general(
        q2_ref[pl.ds(at, rows), :], keys, (((1,), (1,)), ((), ())), preferred_element_type=jnp.float32
    )


def attend_kernel(slots, scale, step, chunk, has_state, final, meta_ref, q_ref, *refs):
    sources = len(slots)
    k_refs, v_refs = refs[:sources], refs[sources : 2 * sources]
    refs = refs[2 * sources :]
    if has_state:
        state_ref, refs = refs[0], refs[1:]
    out_ref, q2_ref, acc_ref = refs
    pairs = q_ref.shape[0]
    tokens = 2 * pairs

    split_queries(q_ref, q2_ref, scale)
    if has_state:
        acc_ref[...] = state_ref[...]
    else:
        acc_ref[...] = jnp.zeros_like(acc_ref)

    largest = None
    for k_ref in k_refs:
        top = jnp.max(jnp.abs(k_ref[...]).astype(jnp.float32), axis=0, keepdims=True)
        largest = top if largest is None else jnp.maximum(largest, top)
    largest = jnp.maximum(largest, swapped(jnp.broadcast_to(largest, (8, LANES)))[:1])
    weighted = jnp.abs(q_ref[...].astype(jnp.float32)) * largest
    row = lax.broadcasted_iota(jnp.int32, (LANES, LANES), 0) < LANES // 2
    col = lax.broadcasted_iota(jnp.int32, (LANES, LANES), 1) < LANES // 2
    same = (row == col).astype(jnp.bfloat16)
    bound = jnp.max(jnp.dot(weighted.astype(jnp.bfloat16), same, preferred_element_type=jnp.float32)) * scale
    safe = bound * 1.02 < 100.0
    if has_state:
        safe = safe & (jnp.max(jnp.abs(acc_ref[:, LANES - 8 :])) == 0.0)

    @pl.when(safe)
    def _():
        for slot, k_ref, v_ref in zip(slots, k_refs, v_refs):
            count = meta_ref[slot]

            def body(start, width, k_ref=k_ref, v_ref=v_ref, count=count):
                keys = key_rows(k_ref, start, width)
                values = value_rows(v_ref, start, width, count)
                scores = scores_of(q2_ref, keys, 0, chunk)
                for at in range(0, tokens, chunk):
                    later = scores_of(q2_ref, keys, at + chunk, chunk) if at + chunk < tokens else None
                    weights = jnp.exp2(scores).astype(jnp.bfloat16)
                    acc_ref[pl.ds(at, chunk), :] += jnp.dot(weights, values, preferred_element_type=jnp.float32)
                    scores = later

            over_tiles(count, pairs, step, body)

    @pl.when(jnp.logical_not(safe))
    def _():
        if not has_state:
            acc_ref[...] = jnp.where(
                lax.broadcasted_iota(jnp.int32, acc_ref.shape, 1) >= 3 * LANES // 4, LOW, 0.0
            )
        rows = min(256, tokens)
        lane = lax.broadcasted_iota(jnp.int32, (rows, LANES), 1)
        for slot, k_ref, v_ref in zip(slots, k_refs, v_refs):
            count = meta_ref[slot]

            def body(start, width, k_ref=k_ref, v_ref=v_ref, count=count):
                keys = key_rows(k_ref, start, width)
                values = value_rows(v_ref, start, width, count)
                at_col = lax.broadcasted_iota(jnp.int32, (rows, 2 * width), 1)
                token = 2 * (start + jnp.where(at_col < width, at_col, at_col - width)) + (at_col >= width)

                def one(i, carry):
                    at = pl.multiple_of(i * rows, rows)
                    scores = jnp.where(token < count, scores_of(q2_ref, keys, at, rows), LOW)
                    old = acc_ref[pl.ds(at, rows), :]
                    before = old[:, LANES - 1 :]
                    top = jnp.maximum(before, jnp.max(scores, axis=1, keepdims=True))
                    weights = jnp.exp2(scores - top).astype(jnp.bfloat16)
                    added = jnp.dot(weights, values, preferred_element_type=jnp.float32)
                    acc_ref[pl.ds(at, rows), :] = jnp.where(
                        lane >= 3 * LANES // 4, top, old * jnp.exp2(before - top) + added
                    )
                    return carry

                lax.fori_loop(0, tokens // rows, one, 0)

            over_tiles(count, pairs, step, body)

    if final:
        lane = lax.broadcasted_iota(jnp.int32, (pairs, LANES), 1)

        def divided(rows):
            sums = jnp.where(lane < 3 * LANES // 4, rows, pltpu.roll(rows, LANES // 4, 1))
            return rows / swapped(sums)

        even, odd = divided(acc_ref[:pairs]), divided(acc_ref[pairs:])
        out_ref[...] = jnp.where(lane < LANES // 2, even, swapped(odd)).astype(out_ref.dtype).reshape(out_ref.shape)
    else:
        out_ref[...] = acc_ref[...]


def attend(meta, queries, within, sources, state, dests, name):
    heads = queries.shape[0]
    pairs = queries.shape[1] // 2
    head_size = LANES // 2
    scale = math.log2(math.e) / math.sqrt(head_size)
    step = min(256, pairs)
    chunk = min(512, 2 * pairs)
    in_specs = [pl.BlockSpec((None, pairs, LANES), lambda h, m: (h, within, 0))]
    arrays = [queries]
    for part in (1, 2):
        for source in sources:
            array, lead, half = source[part]
            if lead is None:
                spec = pl.BlockSpec((None, pairs, LANES), lambda h, m, half=half: (h, half, 0))
            else:
                spec = pl.BlockSpec(
                    (None, None, pairs, LANES), lambda h, m, half=half, lead=lead: (lead, h, half, 0)
                )
            in_specs.append(spec)
            arrays.append(array)
    state_spec = pl.BlockSpec((None, 2 * pairs, LANES), lambda h, m: (h, 0, 0))
    if state is not None:
        in_specs.append(state_spec)
        arrays.append(state)
    if dests is None:
        out_shape = jax.ShapeDtypeStruct((heads, 2 * pairs, LANES), jnp.float32)
        out_spec = state_spec
    else:
        out_shape = jax.ShapeDtypeStruct((dests, heads, pairs // dests, LANES), jnp.bfloat16)
        out_spec = pl.BlockSpec((dests, 1, pairs // dests, LANES), lambda h, m: (0, h, 0, 0))
    slots = tuple(source[0] for source in sources)
    work = heads * len(sources) * (2 * pairs) ** 2
    return pl.pallas_call(
        functools.partial(
            attend_kernel, slots, scale, step, chunk, state is not None, dests is not None
        ),
        out_shape=out_shape,
        grid_spec=pltpu.PrefetchScalarGridSpec(
            num_scalar_prefetch=1,
            grid=(heads,),
            in_specs=in_specs,
            out_specs=out_spec,
            scratch_shapes=[
                pltpu.VMEM((2 * pairs, LANES), jnp.bfloat16),
                pltpu.VMEM((2 * pairs, LANES), jnp.float32),
            ],
        ),
        compiler_params=pltpu.CompilerParams(vmem_limit_bytes=VMEM),
        cost_estimate=pl.CostEstimate(
            flops=work * 4 * head_size * 4, bytes_accessed=8 * heads * pairs * LANES * 2, transcendentals=work
        ),
        name=name,
    )(meta, *arrays)


def project_kernel(layout, rows, weight_ref, *refs):
    parts, out_ref = refs[:-1], refs[-1]
    lane = lax.broadcasted_iota(jnp.int32, (rows, LANES), 1) < LANES // 2
    even, odd = [], []
    for first in range(0, len(layout), 2):
        (p, s, k), (p2, s2, k2) = layout[first], layout[first + 1]
        a = parts[p][s, k].astype(jnp.float32)
        b = parts[p2][s2, k2].astype(jnp.float32)
        even.append(jnp.where(lane, a, swapped(b)).astype(jnp.bfloat16))
        odd.append(jnp.where(lane, swapped(a), b).astype(jnp.bfloat16))
    stacked = jnp.concatenate([jnp.concatenate(even, axis=1), jnp.concatenate(odd, axis=1)], axis=0)
    token = lax.broadcasted_iota(jnp.int32, (2 * rows, 2 * rows), 0)
    place = lax.broadcasted_iota(jnp.int32, (2 * rows, 2 * rows), 1)
    order = (place == token // 2 + (token % 2) * rows).astype(jnp.bfloat16)
    tokens = jnp.dot(order, stacked, preferred_element_type=jnp.float32).astype(jnp.bfloat16)
    out_ref[...] = jnp.dot(tokens, weight_ref[...], preferred_element_type=jnp.float32).astype(out_ref.dtype)


def project(parts, layout, weight):
    pairs = parts[0].shape[2]
    rows = LANES if pairs % LANES == 0 else pairs
    return pl.pallas_call(
        functools.partial(project_kernel, layout, rows),
        out_shape=jax.ShapeDtypeStruct((2 * pairs, weight.shape[1]), jnp.bfloat16),
        grid=(pairs // rows,),
        in_specs=[pl.BlockSpec(weight.shape, lambda i: (0, 0))]
        + [pl.BlockSpec((*part.shape[:2], rows, LANES), lambda i: (0, 0, i, 0)) for part in parts],
        out_specs=pl.BlockSpec((2 * rows, weight.shape[1]), lambda i: (i, 0)),
        compiler_params=pltpu.CompilerParams(vmem_limit_bytes=VMEM),
        name="project",
    )(weight, *parts)


def shifted(x, pairs):
    return lax.ppermute(x, "frame", pairs)


def shards(query_proj, key_proj, value_proj, lengths, out_weight):
    devices = lax.axis_size("frame")
    groups = lax.axis_size("head")
    index = lax.axis_index("frame")
    heads, rows, _ = query_proj.shape
    half = rows // 2
    frames = lengths.shape[0]
    weight = lax.all_gather(out_weight, "head", axis=0, tiled=True)

    odd = index % 2 == 1
    wanted = [2 * index + within - stride for within in range(2) for stride in STRIDES]
    wanted.append(jnp.where(odd, wanted[1], -1))
    wanted.append(jnp.where(odd, -1, wanted[1]))
    wanted = jnp.stack(wanted)
    table = jnp.arange(frames, dtype=jnp.int32)
    meta = jnp.sum(jnp.where(wanted[:, None] == table[None, :], lengths[None, :], 0), axis=1, dtype=jnp.int32)
    meta = jnp.minimum(meta, rows)

    last = jnp.stack((key_proj[:, half:], value_proj[:, half:]))
    first = jnp.stack((key_proj[:, :half], value_proj[:, :half]))
    by_two = [(i, i + 2) for i in range(devices - 2)]
    near_last = shifted(last, by_two)
    prev_odd = shifted(last, [(i, i + 1) for i in range(0, devices - 1, 2)])
    near_first = shifted(first, by_two)
    prev_even = shifted(near_last, [(i + 1, i) for i in range(2, devices - 1, 2)])

    def own(within):
        return (key_proj, None, within), (value_proj, None, within)

    def moved(array):
        return (array, 0, 0), (array, 1, 0)

    state_first = attend(meta, query_proj, 0, [(0, *own(0))], None, None, "first_own")
    state_last = attend(meta, query_proj, 1, [(4, *own(1)), (5, *own(0))], None, None, "last_own")
    sources_last = [(6, *moved(near_last))]
    sources_first = [(8, *moved(prev_odd)), (9, *moved(prev_even)), (2, *moved(near_first))]
    if devices > 8:
        by_eight = [(i, i + 8) for i in range(devices - 8)]
        sources_last.append((7, *moved(shifted(last, by_eight))))
        sources_first.append((3, *moved(shifted(first, by_eight))))
    dests = groups // 2
    out_last = attend(meta, query_proj, 1, sources_last, state_last, dests, "last_rest")
    out_first = attend(meta, query_proj, 0, sources_first, state_first, dests, "first_rest")
    out = jnp.concatenate((out_first, out_last), axis=0)
    got = lax.all_to_all(out, "head", split_axis=0, concat_axis=0, tiled=True)
    layout = tuple((0, head // heads, head % heads) for head in range(groups * heads))
    return project((got,), layout, weight)


def solution(mesh):
    return jax.shard_map(
        shards,
        mesh=mesh,
        in_specs=(
            P("head", "frame", None),
            P("head", "frame", None),
            P("head", "frame", None),
            P(),
            P("head", None),
        ),
        out_specs=P(("frame", "head"), None),
        check_vma=False,
    )
```

time: 800 us -> 330 us (0.41)
  the two profiles are of different devices: /device:TPU:16 before, /device:TPU:10 now
where the time goes in v1:
time: 330 us; the launch traced here: 332 us
  Pallas kernels  272 us (82%)
  waiting for transfers between devices  20.1 us (6%)
  starting transfers between devices  17.2 us (5%)
  between operations  13.6 us (4%)
  local copies, waits for them, and re-layouts  5.17 us (2%)
  other arithmetic  4.04 us (1%)
    pallas_call x4, Pallas kernels, attend(): pl.pallas_call(functools.partial(attend_kernel, slots, scale, step, chunk...  269 us
    all_to_all x1, waiting for transfers between devices, shards(): got = lax.all_to_all(out, 'head', split_axis=0, concat_axis=0, tiled=True)  20 us
    ppermute x4, starting transfers between devices, shifted(): return lax.ppermute(x, 'frame', pairs)  13.6 us
  transfers between devices with their start and end apart: 6, of which 1 were waited for; matrix products, arithmetic and copies ran while one was open for 1% of the time, Pallas kernels for 81%

profile of v1, /device:TPU:10, one launch (start us, length us, event | category | flops | bytes accessed | tf_op | source)
XLA Modules:
  0.0 332.4 jit_solution(4717951175540115938)
XLA Ops:
  6.5 0.0 all-gather.2.cloned.1.call-start
  6.5 2.1 slice_bitcast_fusion
  8.6 1.3 pad_maximum_fusion
  9.9 3.5 %collective-permute-start.1 = (bf16[2,4,768,128]{3,2,1,0:T(8,128)(2,1)}, bf16[2,4,768,128]{3,2,1,0:T(8,128)(2,1)}, u32[]{:S(2)}, u32[]{:S(2)}) collective-permute-start(bf16[2,4,768,128]{3,2,1,0:T(8,128)(2,1)} %pad_maximum_fusion), channel_id=1, source_target_pairs={{0,8},{4,12},{8,16},{12,20},{16,24},{20,28},{1,9},{5,13},{9,17},{1... | collective-permute-start | bytes 4718600 | tf_op jit(solution)/shard_map/ppermute | solution.py:261
  13.4 1.3 collective-permute-start
  14.7 0.0 copy-start.4
  14.7 0.0 copy-start.1
  14.7 0.0 copy-start.2
  14.7 1.3 pad_maximum_fusion.1
  16.0 3.6 %collective-permute-start.3 = (bf16[2,4,768,128]{3,2,1,0:T(8,128)(2,1)}, bf16[2,4,768,128]{3,2,1,0:T(8,128)(2,1)}, u32[]{:S(2)}, u32[]{:S(2)}) collective-permute-start(bf16[2,4,768,128]{3,2,1,0:T(8,128)(2,1)} %pad_maximum_fusion.1), channel_id=1, source_target_pairs={{0,8},{4,12},{8,16},{12,20},{16,24},{20,28},{1,9},{5,13},{9,17},{1... | collective-permute-start | bytes 4718600 | tf_op jit(solution)/shard_map/ppermute | solution.py:261
  19.6 0.0 all-gather.2.cloned.1.call-update
  19.7 0.1 stack.58
  19.7 0.0 copy-done.4
  19.8 0.2 select_reduce_fusion
  19.9 0.0 copy-done.1
  20.0 0.0 copy-start.3
  20.0 1.4 copy-done.3
  21.4 76.7 %last_own.1.refs_2_ = f32[4,1536,128]{2,1,0:T(8,128)} custom-call(s32[10]{0:T(128)S(1)} %broadcast_minimum_fusion.meta_ref, bf16[4,1536,128]{2,1,0:T(8,128)(2,1)S(1)} %copy-done.3, bf16[4,1536,128]{2,1,0:T(8,128)(2,1)S(1)} %copy-done.2, bf16[4,1536,128]{2,1,0:T(8,128)(2,1)S(1)} %copy-done.2, bf16[4,1536,128]{2,1,0:T(8,128)(2,1)S(1)} %copy-done.1, ...), custom_call_target="tpu_custom_call" | custom-call | flops 19327352832 | bytes 6291456 | tf_op jit(solution)/shard_map/last_own/pallas_call | solution.py:204
  98.1 0.0 collective-permute-done.1.refs_0_.refs_1_
  98.1 5.2 %collective-permute-start.2 = (bf16[2,4,768,128]{3,2,1,0:T(8,128)(2,1)}, bf16[2,4,768,128]{3,2,1,0:T(8,128)(2,1)S(1)}, u32[]{:S(2)}, u32[]{:S(2)}) collective-permute-start(bf16[2,4,768,128]{3,2,1,0:T(8,128)(2,1)} %collective-permute-done.1.refs_0_.refs_1_), channel_id=1, source_target_pairs={{12,8},{20,16},{28,24},{13,9},{21,17},{29,25},{14,10},{22,18},{30,... | collective-permute-start | bytes 4718600 | tf_op jit(solution)/shard_map/ppermute | solution.py:261
  103.3 47.2 %first_own.1.refs_6_ = f32[4,1536,128]{2,1,0:T(8,128)} custom-call(s32[10]{0:T(128)S(1)} %broadcast_minimum_fusion.meta_ref, bf16[4,1536,128]{2,1,0:T(8,128)(2,1)S(1)} %copy-done.3, bf16[4,1536,128]{2,1,0:T(8,128)(2,1)S(1)} %copy-done.2, bf16[4,1536,128]{2,1,0:T(8,128)(2,1)S(1)} %copy-done.1), custom_call_target="tpu_custom_call" | custom-call | flops 9663676416 | bytes 6291456 | tf_op jit(solution)/shard_map/first_own/pallas_call | solution.py:204
  150.5 50.4 %last_rest.1 = bf16[2,4,384,128]{3,2,1,0:T(8,128)(2,1)S(1)} custom-call(s32[10]{0:T(128)S(1)} %broadcast_minimum_fusion.meta_ref, bf16[4,1536,128]{2,1,0:T(8,128)(2,1)S(1)} %copy-done.3, bf16[2,4,768,128]{3,2,1,0:T(8,128)(2,1)} %collective-permute-done.1.refs_0_.refs_1_, bf16[2,4,768,128]{3,2,1,0:T(8,128)(2,1)} %collective-permute-done.1.refs_0_.refs_1_, ...), custom_call_target="tpu_custom_call" | custom-call | flops 9663676416 | bytes 6291456 | tf_op jit(solution)/shard_map/last_rest/pallas_call | solution.py:204
  200.8 0.0 collective-permute-done.refs_0_.refs_3_
  200.9 0.0 collective-permute-done.3.refs_2_.refs_5_
  200.9 0.0 collective-permute-done.2.refs_1_.refs_4_
  200.9 94.3 %first_rest.1 = bf16[2,4,384,128]{3,2,1,0:T(8,128)(2,1)S(1)} custom-call(s32[10]{0:T(128)S(1)} %broadcast_minimum_fusion.meta_ref, bf16[4,1536,128]{2,1,0:T(8,128)(2,1)S(1)} %copy-done.3, bf16[2,4,768,128]{3,2,1,0:T(8,128)(2,1)} %collective-permute-done.refs_0_.refs_3_, bf16[2,4,768,128]{3,2,1,0:T(8,128)(2,1)S(1)} %collective-permute-done.2.refs_1_.refs_4_, ...), custom_call_target="tpu_custom_call" | custom-call | flops 28991029248 | bytes 6291456 | tf_op jit(solution)/shard_map/first_rest/pallas_call | solution.py:204
  295.2 1.3 pad_maximum_fusion.2
  296.4 3.6 %all-to-all-start = ((bf16[4,4,384,128]{3,2,1,0:T(8,128)(2,1)}), bf16[4,4,384,128]{3,2,1,0:T(8,128)(2,1)S(1)}, u32[]{:S(2)}, u32[]{:S(2)}) async-start(bf16[4,4,384,128]{3,2,1,0:T(8,128)(2,1)} %pad_maximum_fusion.2), calls=%async_computation | async-start | bytes 3145728 | tf_op jit(solution)/shard_map/all_to_all | solution.py:308
  300.0 0.0 all-gather.2.cloned.1.call-done.weight_ref
  300.0 20.0 %all-to-all-done.refs_0_ = bf16[4,4,384,128]{3,2,1,0:T(8,128)(2,1)S(1)} async-done(((bf16[4,4,384,128]{3,2,1,0:T(8,128)(2,1)}), bf16[4,4,384,128]{3,2,1,0:T(8,128)(2,1)S(1)}, u32[]{:S(2)}, u32[]{:S(2)}) %all-to-all-start) | async-done | bytes 1572896 | tf_op jit(solution)/shard_map/all_to_all | solution.py:308
  320.1 1.6 copy-done
  321.7 3.9 %project.1 = bf16[768,1024]{1,0:T(8,128)(2,1)} custom-call(bf16[1024,1024]{1,0:T(8,128)(2,1)S(1)} %copy-done, bf16[4,4,384,128]{3,2,1,0:T(8,128)(2,1)S(1)} %all-to-all-done.refs_0_), custom_call_target="tpu_custom_call" | custom-call | tf_op jit(solution)/shard_map/project/pallas_call | solution.py:248
  (3 shorter events, 0.0 us)
Async XLA Ops:
  6.5 293.5 %all-gather.2.cloned.1.call-start = ((), (), s32[]{:S(2)}) async-start(), calls=%async_computation.1 | async-start | bytes 2621440 | tf_op jit(solution)/shard_map/all_gather | solution.py:271
  9.9 88.2 %collective-permute-start.1 = (bf16[2,4,768,128]{3,2,1,0:T(8,128)(2,1)}, bf16[2,4,768,128]{3,2,1,0:T(8,128)(2,1)}, u32[]{:S(2)}, u32[]{:S(2)}) collective-permute-start(bf16[2,4,768,128]{3,2,1,0:T(8,128)(2,1)} %pad_maximum_fusion), channel_id=1, source_target_pairs={{0,8},{4,12},{8,16},{12,20},{16,24},{20,28},{1,9},{5,13},{9,17},{1... | collective-permute-start | bytes 4718600 | tf_op jit(solution)/shard_map/ppermute | solution.py:261
  13.4 187.5 %collective-permute-start = (bf16[2,4,768,128]{3,2,1,0:T(8,128)(2,1)}, bf16[2,4,768,128]{3,2,1,0:T(8,128)(2,1)}, u32[]{:S(2)}, u32[]{:S(2)}) collective-permute-start(bf16[2,4,768,128]{3,2,1,0:T(8,128)(2,1)} %pad_maximum_fusion), channel_id=1, source_target_pairs={{0,4},{8,12},{16,20},{24,28},{1,5},{9,13},{17,21},{25,29},{2,6},{1... | collective-permute-start | bytes 4718600 | tf_op jit(solution)/shard_map/ppermute | solution.py:261
  14.7 5.1 %copy-start.4 = (s32[16]{0:T(128)S(1)}, s32[16]{0:T(128)}, u32[]{:S(2)}) copy-start(s32[16]{0:T(128)} %param.8) | copy-start | bytes 196
  14.7 5.3 %copy-start.1 = (bf16[4,1536,128]{2,1,0:T(8,128)(2,1)S(1)}, bf16[4,1536,128]{2,1,0:T(8,128)(2,1)}, u32[]{:S(2)}) copy-start(bf16[4,1536,128]{2,1,0:T(8,128)(2,1)} %refs_3_.1) | copy-start | bytes 4718596
  14.7 5.3 %copy-start.2 = (bf16[4,1536,128]{2,1,0:T(8,128)(2,1)S(1)}, bf16[4,1536,128]{2,1,0:T(8,128)(2,1)}, u32[]{:S(2)}) copy-start(bf16[4,1536,128]{2,1,0:T(8,128)(2,1)} %refs_1_.3) | copy-start | bytes 4718596
  16.0 184.9 %collective-permute-start.3 = (bf16[2,4,768,128]{3,2,1,0:T(8,128)(2,1)}, bf16[2,4,768,128]{3,2,1,0:T(8,128)(2,1)}, u32[]{:S(2)}, u32[]{:S(2)}) collective-permute-start(bf16[2,4,768,128]{3,2,1,0:T(8,128)(2,1)} %pad_maximum_fusion.1), channel_id=1, source_target_pairs={{0,8},{4,12},{8,16},{12,20},{16,24},{20,28},{1,9},{5,13},{9,17},{1... | collective-permute-start | bytes 4718600 | tf_op jit(solution)/shard_map/ppermute | solution.py:261
  20.0 1.4 copy-start.3
  98.1 102.8 %collective-permute-start.2 = (bf16[2,4,768,128]{3,2,1,0:T(8,128)(2,1)}, bf16[2,4,768,128]{3,2,1,0:T(8,128)(2,1)S(1)}, u32[]{:S(2)}, u32[]{:S(2)}) collective-permute-start(bf16[2,4,768,128]{3,2,1,0:T(8,128)(2,1)} %collective-permute-done.1.refs_0_.refs_1_), channel_id=1, source_target_pairs={{12,8},{20,16},{28,24},{13,9},{21,17},{29,25},{14,10},{22,18},{30,... | collective-permute-start | bytes 4718600 | tf_op jit(solution)/shard_map/ppermute | solution.py:261
  296.4 23.6 %all-to-all-start = ((bf16[4,4,384,128]{3,2,1,0:T(8,128)(2,1)}), bf16[4,4,384,128]{3,2,1,0:T(8,128)(2,1)S(1)}, u32[]{:S(2)}, u32[]{:S(2)}) async-start(bf16[4,4,384,128]{3,2,1,0:T(8,128)(2,1)} %pad_maximum_fusion.2), calls=%async_computation | async-start | bytes 3145728 | tf_op jit(solution)/shard_map/all_to_all | solution.py:308
  320.1 1.6 copy-start
Sparse Core Ops, SparseCore 0:
  19.8 24.1 all-gather.1
